TPU v7x, 32 devices: a whole 2x2x4 slice. The times are simulated.
32 devices in a mesh: var: 8 (over z, core), blk: 4 (over y, x).
Axes of the slice: x: 2, y: 2, z: 4, core: 2. Of those that a mesh axis runs over, the one named last changes fastest.
Arguments:
- embeddings: float32 [8, 512, 128], P('var', 'blk'), may hold values from -19 to 19, as said below
- spreads: float32 [5], replicated, may hold values from 0.5 to 8
Outputs:
- mmd: float32 [8], P('var')
- gradient: float32 [8, 512, 128], P('var', 'blk')
Inputs may be any that keep to these rules, and one draw needn't show every extreme that they name: `embeddings`: each group has its own scale and mean offset, and each event its own scale.
All inputs are finite; a program needn't handle non-finite values.
Results may differ from a plain program's by a relative error of at most 0.00016.
Values sent between devices are 32-bit elements; how exact they have to be, the bound alone decides.
A program may use at most 64 MiB of HBM per device.

v0:
```python
import jax
import jax.numpy as jnp
from jax import lax
from jax.sharding import PartitionSpec as P

HIGHEST_PRECISION = lax.Precision.HIGHEST


def spread(value, axis, source):
    kept = jnp.where(lax.axis_index(axis) == source, value, 0).astype(value.dtype)
    return lax.psum(kept, axis)


def pair_tile(left_rows, right_rows, gains):
    left_sq = jnp.sum(left_rows * left_rows, axis=1)
    right_sq = jnp.sum(right_rows * right_rows, axis=1)
    inner = lax.dot_general(
        left_rows,
        right_rows,
        (((1,), (1,)), ((), ())),
        precision=HIGHEST_PRECISION,
        preferred_element_type=jnp.float32,
    )
    distance = left_sq[:, None] + right_sq[None, :] - 2.0 * inner
    kernel_total = jnp.zeros_like(distance)
    weights = jnp.zeros_like(distance)
    band_count = gains.shape[0]
    for band_index in range(band_count):
        decayed = jnp.exp(-distance * gains[band_index])
        kernel_total = kernel_total + decayed
        weights = weights + gains[band_index] * decayed
    return (jnp.sum(kernel_total) / band_count, weights / band_count)


def matmul_high(left_rows, right_rows):
    return jnp.dot(
        left_rows, right_rows, precision=HIGHEST_PRECISION, preferred_element_type=jnp.float32
    )


def shards(embeddings, spreads):
    own_rows = embeddings[0]
    local_count = own_rows.shape[0]
    feat_width = own_rows.shape[1]
    total_events = local_count * lax.axis_size("blk")
    group_total = lax.axis_size("var")
    group_index = lax.axis_index("var")
    gains = 1.0 / (feat_width * spreads)
    nominal = spread(own_rows, "var", 0)
    block_rows = lax.all_gather(own_rows, "blk", axis=0, tiled=True)
    tile_sum, self_w = pair_tile(own_rows, block_rows, gains)
    cross_tile, cross_w = pair_tile(nominal, block_rows, gains)
    updated = (
        tile_sum,
        jnp.sum(self_w, axis=1),
        matmul_high(self_w, block_rows),
        cross_tile,
        jnp.sum(cross_w, axis=1),
        matmul_high(cross_w, block_rows),
    )
    state = (updated, cross_w)[0]
    block_rows = lax.all_gather(nominal, "blk", axis=0, tiled=True)
    unused_sum, pair_w = pair_tile(own_rows, block_rows, gains)
    weight_rows = jnp.sum(pair_w, axis=1)
    weight_mix = matmul_high(pair_w, block_rows)
    member_part = -2.0 * (weight_rows[:, None] * own_rows - weight_mix)
    self_sum, self_rows, self_mix, cross_sum, cross_rows, cross_mix = state
    self_grad = -4.0 * (self_rows[:, None] * own_rows - self_mix)
    nominal_part = -2.0 * (cross_rows[:, None] * nominal - cross_mix)
    is_nominal = group_index == 0
    own_term = jnp.where(is_nominal, (group_total - 1) * self_grad, -2.0 * nominal_part)
    nominal_grad = lax.psum(own_term, "var")
    scale = feat_width / total_events
    gradient = scale * jnp.where(is_nominal, nominal_grad, self_grad - 2.0 * member_part)
    own_self, own_cross = lax.psum((self_sum, cross_sum), "blk")
    nominal_self = spread(own_self, "var", 0)
    mmd = (own_self + nominal_self - 2.0 * own_cross) / (total_events * total_events)
    return (mmd.reshape(1), gradient[None])


def solution(mesh):
    placed = (P("var", "blk", None), P())
    return jax.shard_map(
        shards,
        mesh=mesh,
        in_specs=placed,
        out_specs=(P("var"), P("var", "blk", None)),
        check_vma=False,
    )
```

profile of v0, /device:TPU:0, one launch (start us, length us, event | category | flops | bytes accessed | tf_op | source)
XLA Modules:
  0.0 139.7 jit_solution(5950456403169016713)
XLA Ops:
  7.2 0.0 all-reduce.4.cloned.1.call-start
  7.2 1.5 %bitcast_select_fusion = (f32[128,128]{1,0:T(8,128)}, f32[128]{0:T(128)S(1)}) fusion(f32[1,128,128]{2,1,0:T(8,128)} %param.2, pred[]{:T(512)S(6)} %eq.2), kind=kLoop, calls=%fused_computation.44 | loop fusion | flops 49024 | bytes 131585 | tf_op jit(solution)/shard_map/jit(_where)/select_n | solution.py:10
  8.7 0.0 copy-start
  8.7 0.0 all-reduce.4.cloned.1.call-update
  8.7 0.0 copy-start.2
  8.7 0.0 all-reduce.6.cloned.1.call-start
  8.8 0.8 copy-done
  9.5 10.4 %all-gather = f32[1,512,128]{2,1,0:T(8,128)S(1)} all-gather(f32[1,128,128]{2,1,0:T(8,128)S(1)} %copy-done), channel_id=2, replica_groups=mesh['var'=8,'blk'=4] {'blk'}, dimensions={1}, use_global_device_ids=true | all-gather | bytes 327680 | tf_op jit(solution)/shard_map/all_gather | solution.py:50
  20.0 0.0 copy-done.2
  20.0 0.7 fusion.24
  20.7 0.1 fusion.18
  20.8 4.4 %fusion.22 = (f32[128]{0:T(128)S(1)}, f32[]{:T(128)}, f32[128,512]{1,0:T(8,128)S(1)}) fusion(f32[]{:T(128)} %bitcast.6, f32[]{:T(128)} %bitcast.5, f32[]{:T(128)} %bitcast.4, f32[]{:T(128)} %bitcast.3, f32[]{:T(128)} %bitcast.2, f32[1,512,128]{2,1,0:T(8,128)S(1)} %all-gather, f32[1,128,128]{2,1,0:T(8,128)S(1)} %copy-done, f32[512]{0:T(512)S(1)} %fusion.18, ...), kind=kOutput, calls=%fused_computation.51 | convolution fusion | flops 102301568 | bytes 592920 | tf_op jit(solution)/shard_map/dot_general | solution.py:17
  25.2 3.7 %convolution_subtract_fusion.2 = f32[128,128]{1,0:T(8,128)S(1)} fusion(f32[1,512,128]{2,1,0:T(8,128)S(1)} %all-gather, f32[1,128,128]{2,1,0:T(8,128)S(1)} %copy-done, f32[128]{0:T(128)S(1)} %get-tuple-element.4, f32[128,512]{1,0:T(8,128)S(1)} %get-tuple-element.15, f32[]{:T(128)} %bitcast.6, f32[]{:T(128)} %bitcast.5, f32[]{:T(128)} %bitcast.4, ...), kind=kOutput, calls=%fused_computation.12 | convolution fusion | flops 101679104 | bytes 655892 | tf_op jit(solution)/shard_map/dot_general | solution.py:36
  29.5 37.7 %all-reduce.4.cloned.1.call-done = f32[128,128]{1,0:T(8,128)} async-done(((f32[128,128]{1,0:T(8,128)}), f32[128,128]{1,0:T(8,128)}) %all-reduce.4.cloned.1.call-update) | async-done | bytes 65552 | tf_op jit(solution)/shard_map/psum | solution.py:11
  67.2 0.0 copy-start.1
  67.2 1.0 multiply_reduce_fusion.1
  68.2 0.0 copy-done.1
  68.3 4.4 %fusion.23 = (f32[128]{0:T(128)S(1)}, f32[]{:T(128)}, f32[128,512]{1,0:T(8,128)S(1)}) fusion(f32[]{:T(128)} %bitcast.6, f32[]{:T(128)} %bitcast.5, f32[]{:T(128)} %bitcast.4, f32[]{:T(128)} %bitcast.3, f32[]{:T(128)} %bitcast.2, f32[128,128]{1,0:T(8,128)S(1)} %copy-done.1, f32[1,512,128]{2,1,0:T(8,128)S(1)} %all-gather, f32[512]{0:T(512)S(1)} %fusion.18, ...), kind=kOutput, calls=%fused_computation.52 | convolution fusion | flops 102301568 | bytes 592920 | tf_op jit(solution)/shard_map/dot_general | solution.py:17
  72.6 4.4 %fusion.8 = f32[128,128]{1,0:T(8,128)} fusion(f32[1,512,128]{2,1,0:T(8,128)S(1)} %all-gather, f32[128,128]{1,0:T(8,128)S(1)} %copy-done.1, f32[128,128]{1,0:T(8,128)S(1)} %convolution_subtract_fusion.2, f32[128]{0:T(128)S(1)} %get-tuple-element.2, pred[]{:T(512)S(6)} %eq.2, f32[128,512]{1,0:T(8,128)S(1)} %get-tuple-element.16, f32[]{:T(128)} %bitcast.6, ...), kind=kOutput, calls=%fused_computation.14 | convolution fusion | flops 101728256 | bytes 721429 | tf_op jit(solution)/shard_map/dot_general | solution.py:36
  77.0 0.0 all-reduce.6.cloned.1.call-update
  77.6 9.3 %all_gather.7 = f32[512,128]{1,0:T(8,128)S(1)} all-gather(f32[128,128]{1,0:T(8,128)S(1)} %copy-done.1), channel_id=1, replica_groups=mesh['var'=8,'blk'=4] {'blk'}, dimensions={0}, use_global_device_ids=true | all-gather | bytes 327680 | tf_op jit(solution)/shard_map/all_gather | solution.py:62
  86.9 0.1 multiply_reduce_fusion
  87.0 9.5 %all-reduce = (f32[]{:T(128)}, f32[]{:T(128)}) all-reduce(f32[]{:T(128)S(6)} %div.22, f32[]{:T(128)S(6)} %div.23), channel_id=1, replica_groups=mesh['var'=8,'blk'=4] {'blk'}, use_global_device_ids=true, to_apply=%region_3.4 | all-reduce | flops 2 | bytes 16 | tf_op jit(solution)/shard_map/psum | solution.py:75
  97.1 3.8 %fusion.25 = (f32[128]{0:T(128)S(1)}, f32[128,512]{1,0:T(8,128)S(1)}) fusion(f32[]{:T(128)} %bitcast.6, f32[]{:T(128)} %bitcast.5, f32[]{:T(128)} %bitcast.4, f32[]{:T(128)} %bitcast.3, f32[512,128]{1,0:T(8,128)S(1)} %all_gather.7, f32[1,128,128]{2,1,0:T(8,128)S(1)} %copy-done, f32[512]{0:T(512)S(1)} %multiply_reduce_fusion, f32[128]{0:T(128)S(1)} %get-tuple-element.9, ...), kind=kOutput, calls=%fused_computation.54 | convolution fusion | flops 101973888 | bytes 592916 | tf_op jit(solution)/shard_map/dot_general | solution.py:17
  101.0 14.1 %psum.36 = f32[]{:T(128)} all-reduce(f32[]{:T(128)S(6)} %select_n.22), channel_id=1, replica_groups=mesh['var'=8,'blk'=4] {'var'}, use_global_device_ids=true, to_apply=%region_4.5 | all-reduce | flops 1 | bytes 8 | tf_op jit(solution)/shard_map/psum | solution.py:11
  116.9 12.9 %all-reduce.6.cloned.1.call-done = f32[128,128]{1,0:T(8,128)} async-done(((f32[128,128]{1,0:T(8,128)}), f32[128,128]{1,0:T(8,128)}) %all-reduce.6.cloned.1.call-update) | async-done | bytes 65552 | tf_op jit(solution)/shard_map/psum | solution.py:72
  129.8 1.9 %fusion.13 = f32[1,128,128]{2,1,0:T(8,128)} fusion(f32[128,128]{1,0:T(8,128)} %all-reduce.6.cloned.1.call-done, f32[128,512]{1,0:T(8,128)S(1)} %get-tuple-element.18, f32[512,128]{1,0:T(8,128)S(1)} %all_gather.7, f32[1,128,128]{2,1,0:T(8,128)S(1)} %copy-done, f32[128,128]{1,0:T(8,128)S(1)} %convolution_subtract_fusion.2, f32[128]{0:T(128)S(1)} %get-tuple-element.17, ...), kind=kOutput, calls=%fused_computation.19 | convolution fusion | flops 100777984 | bytes 786945 | tf_op jit(solution)/shard_map/dot_general | solution.py:36
  (1 shorter events, 0.0 us)
Async XLA Ops:
  7.2 60.1 %all-reduce.4.cloned.1.call-start = ((), (), s32[]{:S(2)}) async-start(), calls=%async_computation | async-start | bytes 131072 | tf_op jit(solution)/shard_map/psum | solution.py:11
  8.7 0.8 copy-start
  8.7 11.2 %copy-start.2 = (f32[5]{0:T(128)S(1)}, f32[5]{0:T(128)}, u32[]{:S(2)}) copy-start(f32[5]{0:T(128)} %param.3) | copy-start | bytes 64
  8.7 121.1 %all-reduce.6.cloned.1.call-start = ((), (), s32[]{:S(2)}) async-start(), calls=%async_computation.1 | async-start | bytes 131072 | tf_op jit(solution)/shard_map/psum | solution.py:72
  67.2 1.0 copy-start.1
Sparse Core Ops, SparseCore 0:
  10.9 56.3 all-reduce.3
  77.2 52.6 all-reduce.5
where the time goes:
time: 140 us
  waiting for transfers between devices  50.6 us (36%)
  blocking collectives  43.3 us (31%)
  matrix products  22.6 us (16%)
  between operations  18.8 us (13%)
  other arithmetic  2.78 us (2%)
  local copies, waits for them, and re-layouts  1.44 us (1%)
    psum x1, waiting for transfers between devices, spread(): return lax.psum(kept, axis)  37.7 us
    psum x1, blocking collectives, spread(): return lax.psum(kept, axis)  14.1 us
    psum x1, waiting for transfers between devices, shards(): nominal_grad = lax.psum(own_term, 'var')  12.9 us
    dot_general x3, matrix products, pair_tile(): lax.dot_general(left_rows, right_rows, (((1,), (1,)), ((), ())), precisio...  12.6 us
    all_gather x1, blocking collectives, shards(): block_rows = lax.all_gather(own_rows, 'blk', axis=0, tiled=True)  10.4 us
    dot_general x3, matrix products, matmul_high(): jnp.dot(left_rows, right_rows, precision=HIGHEST_PRECISION, preferred_ele...  9.95 us
    psum x1, blocking collectives, shards(): own_self, own_cross = lax.psum((self_sum, cross_sum), 'blk')  9.51 us
    all_gather x1, blocking collectives, shards(): block_rows = lax.all_gather(nominal, 'blk', axis=0, tiled=True)  9.3 us
  transfers between devices with their start and end apart: 2, of which 2 were waited for; matrix products, arithmetic and copies ran while one was open for 9% of the time, Pallas kernels for 0%

commit v1 on v0

v1 whole, which is shorter than its diff:
```python
import functools

import jax
import jax.numpy as jnp
from jax import lax
from jax.experimental import pallas as pl
from jax.experimental.pallas import tpu as pltpu
from jax.sharding import PartitionSpec as P

HIGHEST = lax.Precision.HIGHEST
LOG2E = 1.4426950408889634


def partner(index, step, count):
    result = 0
    bit = 1
    while bit < count:
        result = result + ((index // bit + step // bit) % 2) * bit
        bit *= 2
    return result


def dot_t(left, right):
    return lax.dot_general(
        left, right, (((1,), (1,)), ((), ())), precision=HIGHEST, preferred_element_type=jnp.float32
    )


def dot_n(left, right):
    return lax.dot_general(
        left, right, (((1,), (0,)), ((), ())), precision=HIGHEST, preferred_element_type=jnp.float32
    )


def fold(tile):
    return jnp.sum(tile.reshape(tile.shape[0] // 8, 8, tile.shape[1]), axis=0)


def row_square(rows):
    return jnp.sum(rows * rows, axis=1, keepdims=True)


def col_square(rows):
    return dot_t(jnp.ones((8, rows.shape[1]), jnp.float32), rows * rows)[0:1]


def kernel(
    groups, blocks, bands,
    spread_ref, emb_ref, mmd_ref, grad_ref,
    y_buf, x_buf, t_buf, t_out, s_buf, s_out, m_buf,
    y_send, y_recv, x_send, x_recv, g_send, g_recv, t_send, t_recv, s_send, s_recv, m_send, m_recv,
):
    group = lax.axis_index("var")
    block = lax.axis_index("blk")
    count, width = emb_ref.shape[1], emb_ref.shape[2]
    events = count * blocks
    scale = width / events
    nominal = group == 0
    own_ref = emb_ref.at[0]

    def copy(src, dst, send, recv, var, blk):
        return pltpu.make_async_remote_copy(
            src_ref=src, dst_ref=dst, send_sem=send, recv_sem=recv,
            device_id={"var": var, "blk": blk}, device_id_type=pl.DeviceIdType.MESH,
        )

    def y_copy(step):
        return copy(own_ref, y_buf.at[step - 1], y_send.at[step - 1], y_recv.at[step - 1],
                    group, partner(block, step, blocks))

    def x_copy(var):
        return copy(own_ref, x_buf.at[0], x_send.at[var - 1], x_recv.at[0], var, block)

    def g_copy(step):
        return copy(x_buf.at[0], x_buf.at[step], g_send.at[step - 1], g_recv.at[step - 1],
                    group, partner(block, step, blocks))

    def t_copy(slot):
        return copy(t_out, t_buf.at[slot], t_send.at[0], t_recv.at[slot], 0, block)

    def s_copy(var):
        return copy(s_out, s_buf, s_send.at[var - 1], s_recv.at[0], var, block)

    def m_copy(step):
        return copy(m_buf.at[block], m_buf.at[block], m_send.at[step - 1], m_recv.at[step - 1],
                    group, partner(block, step, blocks))

    barrier = pltpu.get_barrier_semaphore()

    def greet(var, blk):
        pl.semaphore_signal(barrier, inc=1, device_id={"var": var, "blk": blk},
                            device_id_type=pl.DeviceIdType.MESH)

    for step in range(1, blocks):
        greet(group, partner(block, step, blocks))

    @pl.when(nominal)
    def _():
        for var in range(1, groups):
            greet(var, block)
        pl.semaphore_wait(barrier, blocks - 1 + groups - 1)
        for var in range(groups - 1, 0, -1):
            x_copy(var).start()

    @pl.when(jnp.logical_not(nominal))
    def _():
        greet(0, block)
        pl.semaphore_wait(barrier, blocks)

    for step in range(1, blocks):
        y_copy(step).start()

    gains = [1.0 / (width * jnp.full((1, width), spread_ref[s], jnp.float32)) for s in range(bands)]
    rates = [-LOG2E * gain for gain in gains]
    own = own_ref[...]
    own_row = row_square(own)
    own_col = col_square(own)

    def tile(left, left_row, right, right_col, sums):
        distance = left_row + right_col - 2.0 * dot_t(left, right)
        total = None
        weights = None
        for gain, rate in zip(gains, rates):
            decayed = jnp.exp2(distance * rate)
            weighted = gain * decayed
            weights = weighted if weights is None else weights + weighted
            if sums:
                total = decayed if total is None else total + decayed
        return (fold(total) / bands if sums else None), weights / bands

    def y_block(step):
        return own if step == 0 else y_buf[step - 1]

    self_sum, self_w = tile(own, own_row, own, own_col, True)
    self_mix = dot_n(self_w, own)

    def rest_of_self():
        total, weights, mix = self_sum, self_w, self_mix
        for step in range(1, blocks):
            rows = y_block(step)
            part, w = tile(own, own_row, rows, col_square(rows), True)
            total, weights, mix = total + part, weights + w, mix + dot_n(w, rows)
        return total, -4.0 * (jnp.sum(weights, axis=1, keepdims=True) * own - mix)

    def finish_mmd(part):
        m_buf[block] = part
        for step in range(1, blocks):
            m_copy(step).start()

    def read_mmd():
        for step in range(1, blocks):
            m_copy(step).wait_recv()
        mmd_ref[0] = jnp.sum(jnp.sum(m_buf[...], axis=0)) / (events * events)

    @pl.when(nominal)
    def _():
        for step in range(1, blocks):
            y_copy(step).wait_recv()
        total, self_grad = rest_of_self()
        s_out[...] = total
        for var in range(1, groups):
            s_copy(var).start()
        finish_mmd(total + total - 2.0 * total)
        grad = (groups - 1) * self_grad
        grad_ref[0] = grad
        read_mmd()
        for var in range(1, groups):
            t_copy(var - 1).wait_recv()
            grad = grad - 2.0 * t_buf[var - 1]
        grad_ref[0] = scale * grad
        for var in range(1, groups):
            x_copy(var).wait_send()
            s_copy(var).wait_send()

    @pl.when(jnp.logical_not(nominal))
    def _():
        x_copy(group).wait_recv()
        for step in range(1, blocks):
            g_copy(step).start()
        for step in range(1, blocks):
            y_copy(step).wait_recv()
        anchor = x_buf[0]
        anchor_row = row_square(anchor)
        total = weights = mix = None
        for step in range(blocks):
            rows = y_block(step)
            part, w = tile(anchor, anchor_row, rows, own_col if step == 0 else col_square(rows), True)
            term = dot_n(w, rows)
            if step == 0:
                total, weights, mix = part, w, term
            else:
                total, weights, mix = total + part, weights + w, mix + term
        t_out[...] = -2.0 * (jnp.sum(weights, axis=1, keepdims=True) * anchor - mix)
        t_copy(group - 1).start()
        self_total, self_grad = rest_of_self()
        s_copy(group).wait_recv()
        finish_mmd(self_total + s_buf[...] - 2.0 * total)
        for step in range(blocks):
            if step:
                g_copy(step).wait_recv()
            rows = x_buf[step]
            _, w = tile(own, own_row, rows, col_square(rows), False)
            term = dot_n(w, rows)
            weights, mix = (w, term) if step == 0 else (weights + w, mix + term)
        member = -2.0 * (jnp.sum(weights, axis=1, keepdims=True) * own - mix)
        grad_ref[0] = scale * (self_grad - 2.0 * member)
        read_mmd()
        for step in range(1, blocks):
            g_copy(step).wait_send()
        t_copy(group - 1).wait_send()

    for step in range(1, blocks):
        y_copy(step).wait_send()
        m_copy(step).wait_send()


def solution(mesh):
    groups, blocks = mesh.shape["var"], mesh.shape["blk"]

    def shards(embeddings, spreads):
        _, count, width = embeddings.shape
        bands = spreads.shape[0]
        dma = pltpu.SemaphoreType.DMA
        f32 = jnp.float32
        return pl.pallas_call(
            functools.partial(kernel, groups, blocks, bands),
            out_shape=(jax.ShapeDtypeStruct((1,), f32), jax.ShapeDtypeStruct((1, count, width), f32)),
            in_specs=[pl.BlockSpec(memory_space=pltpu.SMEM), pl.BlockSpec(memory_space=pltpu.VMEM)],
            out_specs=(pl.BlockSpec(memory_space=pltpu.SMEM), pl.BlockSpec(memory_space=pltpu.VMEM)),
            scratch_shapes=[
                pltpu.VMEM((blocks - 1, count, width), f32),
                pltpu.VMEM((blocks, count, width), f32),
                pltpu.VMEM((groups - 1, count, width), f32),
                pltpu.VMEM((count, width), f32),
                pltpu.VMEM((8, width), f32),
                pltpu.VMEM((8, width), f32),
                pltpu.VMEM((blocks, 8, width), f32),
                dma((blocks - 1,)), dma((blocks - 1,)),
                dma((groups - 1,)), dma((1,)),
                dma((blocks - 1,)), dma((blocks - 1,)),
                dma((1,)), dma((groups - 1,)),
                dma((groups - 1,)), dma((1,)),
                dma((blocks - 1,)), dma((blocks - 1,)),
            ],
            compiler_params=pltpu.CompilerParams(
                collective_id=0, has_side_effects=True, vmem_limit_bytes=32 * 1024 * 1024
            ),
        )(spreads, embeddings)

    return jax.shard_map(
        shards,
        mesh=mesh,
        in_specs=(P("var", "blk", None), P()),
        out_specs=(P("var"), P("var", "blk", None)),
        check_vma=False,
    )
```

time: 140 us -> 24.1 us (0.17)
  waiting for transfers between devices: 50.6 us -> 0 us
  blocking collectives: 43.3 us -> 0 us
  matrix products: 22.6 us -> 0 us
  Pallas kernels: 0 us -> 19.4 us
  between operations: 18.8 us -> 2.41 us
  other arithmetic: 2.78 us -> 0 us
    psum x2 -> x0, waiting for transfers between devices: 50.6 us -> none  [the longest x1 37.7 us: spread(): return lax.psum(kept, axis)]
    psum x2 -> x0, blocking collectives: 23.6 us -> none  [the longest x1 14.1 us: spread(): return lax.psum(kept, axis)]
    dot_general x6 -> x0, matrix products: 22.6 us -> none  [the longest x3 12.6 us: pair_tile(): lax.dot_general(left_rows, right_rows, (((1,), (1,)), ((), ())), precisio...]
    all_gather x2 -> x0, blocking collectives: 19.7 us -> none  [the longest x1 10.4 us: shards(): block_rows = lax.all_gather(own_rows, 'blk', axis=0, tiled=True)]
    pallas_call x0 -> x1, Pallas kernels: none -> 19.4 us  [shards(): pl.pallas_call(functools.partial(kernel, groups, blocks, bands), out_shap...]
    select_n x1 -> x0, other arithmetic: 1.48 us -> none  [spread(): jnp.where(lax.axis_index(axis) == source, value, 0).astype(value.dtype)]
  transfers between devices with their start and end apart: 2 -> 0, of which waited for: 2 -> 0; matrix products, arithmetic and copies ran while one was open for 9% -> 0% of each run, Pallas kernels for 0% -> 0%
where the time goes in v1:
time: 24.1 us; the launch traced here: 24 us
  Pallas kernels  19.4 us (80%)
  between operations  2.41 us (10%)
  local copies, waits for them, and re-layouts  2.12 us (9%)
    pallas_call x1, Pallas kernels, shards(): pl.pallas_call(functools.partial(kernel, groups, blocks, bands), out_shap...  19.4 us
    unnamed x5, local copies, waits for them, and re-layouts  2.12 us

profile of v1, /device:TPU:0, one launch (start us, length us, event | category | flops | bytes accessed | tf_op | source)
XLA Modules:
  0.0 24.0 jit_solution(18260157228923115316)
XLA Ops:
  0.6 0.0 copy-start
  0.6 0.8 %copy-done = f32[1,128,128]{2,1,0:T(8,128)S(1)} copy-done((f32[1,128,128]{2,1,0:T(8,128)S(1)}, f32[1,128,128]{2,1,0:T(8,128)}, u32[]{:S(2)}) %copy-start) | copy-done | bytes 65560
  1.5 0.0 copy-start.1
  1.5 0.7 %copy-done.1 = f32[5]{0:T(128)S(1)} copy-done((f32[5]{0:T(128)S(1)}, f32[5]{0:T(128)}, u32[]{:S(2)}) %copy-start.1) | copy-done | bytes 44
  2.1 19.4 %shard_map.41 = (f32[1]{0:T(128)}, f32[1,128,128]{2,1,0:T(8,128)S(1)}) custom-call(f32[5]{0:T(128)S(1)} %copy-done.1, f32[1,128,128]{2,1,0:T(8,128)S(1)} %copy-done), custom_call_target="tpu_custom_call" | custom-call | tf_op jit(solution)/shard_map/pallas_call | solution.py:225
  22.2 0.6 %copy.7 = f32[1,128,128]{2,1,0:T(8,128)} copy(f32[1,128,128]{2,1,0:T(8,128)S(1)} %get-tuple-element.5) | data formatting | bytes 131072
Async XLA Ops:
  0.6 0.8 %copy-start = (f32[1,128,128]{2,1,0:T(8,128)S(1)}, f32[1,128,128]{2,1,0:T(8,128)}, u32[]{:S(2)}) copy-start(f32[1,128,128]{2,1,0:T(8,128)} %emb_ref.1) | copy-start | bytes 196612
  1.5 0.7 %copy-start.1 = (f32[5]{0:T(128)S(1)}, f32[5]{0:T(128)}, u32[]{:S(2)}) copy-start(f32[5]{0:T(128)} %spread_ref.1) | copy-start | bytes 64

commit v2 on v1

v2 whole, which is shorter than its diff:
```python
import functools

import jax
import jax.numpy as jnp
from jax import lax
from jax.experimental import pallas as pl
from jax.experimental.pallas import tpu as pltpu
from jax.sharding import PartitionSpec as P

HIGHEST = lax.Precision.HIGHEST
LOG2E = 1.4426950408889634
EARLY = 2


def partner(index, step, count):
    result = 0
    bit = 1
    while bit < count:
        result = result + ((index // bit + step // bit) % 2) * bit
        bit *= 2
    return result


def dot_t(left, right):
    return lax.dot_general(
        left, right, (((1,), (1,)), ((), ())), precision=HIGHEST, preferred_element_type=jnp.float32
    )


def dot_n(left, right):
    return lax.dot_general(
        left, right, (((1,), (0,)), ((), ())), precision=HIGHEST, preferred_element_type=jnp.float32
    )


def fold(tile):
    return jnp.sum(tile.reshape(tile.shape[0] // 8, 8, tile.shape[1]), axis=0)


def row_square(rows):
    return jnp.sum(rows * rows, axis=1, keepdims=True)


def col_square(rows):
    return dot_t(jnp.ones((8, rows.shape[1]), jnp.float32), rows * rows)[0:1]


def kernel(
    groups, blocks, bands,
    spread_hbm, emb_hbm, mmd_ref, grad_ref,
    spread_ref, own_ref, y_buf, x_buf, t_buf, t_out, t_mate, s_buf, s_out, m_buf,
    load, y_send, y_recv, x_send, x_recv, n_send, n_recv, w_send, w_recv, g_send, g_recv,
    p_send, p_recv, t_send, t_recv, s_send, s_recv, m_send, m_recv,
):
    group = lax.axis_index("var")
    block = lax.axis_index("blk")
    _, half, width = own_ref.shape
    count = 2 * half
    events = count * blocks
    scale = width / events
    nominal = group == 0
    outer = group >= 2
    chip = group // 2
    core = group % 2
    mate = 2 * chip + 1 - core
    mesh_ids = pl.DeviceIdType.MESH

    def peer(step):
        return partner(block, step, blocks)

    def copy(src, dst, send, recv, var, blk):
        return pltpu.make_async_remote_copy(
            src_ref=src, dst_ref=dst, send_sem=send, recv_sem=recv,
            device_id={"var": var, "blk": blk}, device_id_type=mesh_ids,
        )

    load_own = pltpu.make_async_copy(emb_hbm.at[0], own_ref, load.at[0])
    load_spread = pltpu.make_async_copy(spread_hbm, spread_ref, load.at[1])
    load_own.start()
    load_spread.start()

    def y_copy(step):
        return copy(own_ref, y_buf.at[step - 1], y_send.at[step - 1], y_recv.at[step - 1], group, peer(step))

    def x_copy(var, part):
        return copy(own_ref.at[part], x_buf.at[0, part], x_send.at[var - 2], x_recv.at[0], var, block)

    def n_copy(step):
        return copy(own_ref, x_buf.at[step], n_send.at[step], n_recv.at[step], 1, peer(step))

    def w_copy(part):
        return copy(x_buf.at[0, part], x_buf.at[0, part], w_send.at[0], w_recv.at[0], mate, block)

    def g_copy(step, part, other):
        return copy(x_buf.at[0, part], x_buf.at[step, part], g_send.at[2 * step - 2 + other],
                    g_recv.at[2 * step - 2 + part], mate if other else group, peer(step))

    def p_copy():
        return copy(t_out.at[core], t_mate, p_send.at[0], p_recv.at[0], mate, block)

    def t_copy(source, part):
        return copy(t_out.at[part], t_buf.at[source, part], t_send.at[part], t_recv.at[2 * source + part], 0, block)

    def s_copy(var):
        return copy(s_out, s_buf, s_send.at[var - 1], s_recv.at[0], var, block)

    def m_copy(step):
        return copy(m_buf.at[block], m_buf.at[block], m_send.at[step - 1], m_recv.at[step - 1], group, peer(step))

    barrier = pltpu.get_barrier_semaphore()

    def greet(var, blk):
        pl.semaphore_signal(barrier, inc=1, device_id={"var": var, "blk": blk}, device_id_type=mesh_ids)

    @pl.when(outer)
    def _():
        greet(0, block)

    @pl.when(nominal)
    def _():
        for var in range(groups - 1, 1, -1):
            greet(var, block)

    greet(mate, block)
    for step in range(1, blocks):
        greet(group, peer(step))
        greet(mate, peer(step))

    @pl.when(nominal)
    def _():
        pl.semaphore_wait(barrier, 2 * blocks - 1 + groups - 2)
        load_own.wait()
        for var in range(groups - 1, 1, -1):
            x_copy(var, var % 2).start()
        n_copy(0).start()

    @pl.when(group == 1)
    def _():
        pl.semaphore_wait(barrier, 2 * blocks - 1)
        load_own.wait()

    @pl.when(outer)
    def _():
        pl.semaphore_wait(barrier, 2 * blocks)
        load_own.wait()

    for step in range(1, blocks):
        y_copy(step).start()

    @pl.when(nominal)
    def _():
        for step in range(1, blocks):
            n_copy(step).start()

    load_spread.wait()
    gains = [1.0 / (width * jnp.full((1, width), spread_ref[s], jnp.float32)) for s in range(bands)]
    rates = [-LOG2E * gain for gain in gains]

    def whole(rows):
        return rows.reshape(count, width)

    own = whole(own_ref[...])
    own_row = row_square(own)
    own_col = col_square(own)

    def tile(left, left_row, right, right_col, sums):
        distance = left_row + right_col - 2.0 * dot_t(left, right)
        total = None
        weights = None
        for gain, rate in zip(gains, rates):
            decayed = jnp.exp2(distance * rate)
            weighted = gain * decayed
            weights = weighted if weights is None else weights + weighted
            if sums:
                total = decayed if total is None else total + decayed
        return (fold(total) / bands if sums else None), weights / bands

    def y_block(step):
        return own if step == 0 else whole(y_buf[step - 1])

    def y_col(step):
        return own_col if step == 0 else col_square(y_block(step))

    def add(state, term):
        return term if state is None else tuple(a + b for a, b in zip(state, term))

    def against_group(left, left_row, steps, state=None, wait=False):
        for step in steps:
            if wait and step:
                y_copy(step).wait_recv()
            rows = y_block(step)
            part, w = tile(left, left_row, rows, y_col(step), True)
            state = add(state, (part, w, dot_n(w, rows)))
        return state

    def difference(weights, rows, mix):
        return jnp.sum(weights, axis=1, keepdims=True) * rows - mix

    self_state = against_group(own, own_row, range(EARLY), None, True)

    def rest_of_self():
        total, weights, mix = against_group(own, own_row, range(EARLY, blocks), self_state)
        return total, -4.0 * difference(weights, own, mix)

    def finish_mmd(part):
        m_buf[block] = part
        for step in range(1, blocks):
            m_copy(step).start()

    def read_mmd():
        for step in range(1, blocks):
            m_copy(step).wait_recv()
        mmd_ref[0] = jnp.sum(jnp.sum(m_buf[...], axis=0)) / (events * events)

    @pl.when(nominal)
    def _():
        for step in range(EARLY, blocks):
            y_copy(step).wait_recv()
        total, self_grad = rest_of_self()
        s_out[...] = total
        for var in range(1, groups):
            s_copy(var).start()
        finish_mmd(total + total - 2.0 * total)
        grad = (groups - 1) * self_grad
        read_mmd()
        for source in range(groups // 2 - 1, -1, -1):
            for part in range(2):
                t_copy(source, part).wait_recv()
            grad = grad - 2.0 * whole(t_buf[source])
        grad_ref[0] = scale * grad
        for var in range(1, groups):
            if var > 1:
                x_copy(var, var % 2).wait_send()
            s_copy(var).wait_send()
        for step in range(blocks):
            n_copy(step).wait_send()

    @pl.when(jnp.logical_not(nominal))
    def _():
        @pl.when(outer)
        def _():
            x_copy(group, core).wait_recv()
            w_copy(core).start()
            for step in range(1, blocks):
                for other in range(2):
                    g_copy(step, core, other).start()

        @pl.when(group == 1)
        def _():
            n_copy(0).wait_recv()

        for step in range(EARLY, blocks):
            y_copy(step).wait_recv()

        def cross(part):
            anchor = x_buf[0, part]
            total, weights, mix = against_group(anchor, row_square(anchor), range(blocks))
            return total, -2.0 * difference(weights, anchor, mix)

        first_total, t_out[core] = cross(core)

        @pl.when(outer)
        def _():
            p_copy().start()
            w_copy(1 - core).wait_recv()

        @pl.when(group == 1)
        def _():
            t_copy(0, core).start()

        second_total, second = cross(1 - core)

        @pl.when(outer)
        def _():
            p_copy().wait_recv()
            t_out[1 - core] = second + t_mate[...]

        @pl.when(group == 1)
        def _():
            t_out[1 - core] = second

        t_copy(chip, 1 - core).start()
        self_total, self_grad = rest_of_self()
        s_copy(group).wait_recv()
        finish_mmd(self_total + s_buf[...] - 2.0 * (first_total + second_total))
        state = None
        for step in range(blocks):
            if step:
                @pl.when(outer)
                def _():
                    for part in range(2):
                        g_copy(step, part, 0).wait_recv()

                @pl.when(group == 1)
                def _():
                    n_copy(step).wait_recv()

            rows = whole(x_buf[step])
            _, w = tile(own, own_row, rows, col_square(rows), False)
            state = add(state, (w, dot_n(w, rows)))
        member = -2.0 * difference(state[0], own, state[1])
        grad_ref[0] = scale * (self_grad - 2.0 * member)
        read_mmd()

        @pl.when(outer)
        def _():
            w_copy(core).wait_send()
            p_copy().wait_send()
            for step in range(1, blocks):
                for other in range(2):
                    g_copy(step, core, other).wait_send()

        @pl.when(group == 1)
        def _():
            t_copy(0, core).wait_send()

        t_copy(chip, 1 - core).wait_send()

    for step in range(1, blocks):
        y_copy(step).wait_send()
        m_copy(step).wait_send()


def solution(mesh):
    groups, blocks = mesh.shape["var"], mesh.shape["blk"]

    def shards(embeddings, spreads):
        _, count, width = embeddings.shape
        half = count // 2
        bands = spreads.shape[0]
        dma = pltpu.SemaphoreType.DMA
        f32 = jnp.float32
        mmd, gradient = pl.pallas_call(
            functools.partial(kernel, groups, blocks, bands),
            out_shape=(jax.ShapeDtypeStruct((1,), f32), jax.ShapeDtypeStruct((1, count, width), f32)),
            in_specs=[pl.BlockSpec(memory_space=pltpu.HBM)] * 2,
            out_specs=(pl.BlockSpec(memory_space=pltpu.SMEM), pl.BlockSpec(memory_space=pltpu.VMEM)),
            scratch_shapes=[
                pltpu.SMEM((bands,), f32),
                pltpu.VMEM((2, half, width), f32),
                pltpu.VMEM((blocks - 1, 2, half, width), f32),
                pltpu.VMEM((blocks, 2, half, width), f32),
                pltpu.VMEM((groups // 2, 2, half, width), f32),
                pltpu.VMEM((2, half, width), f32),
                pltpu.VMEM((half, width), f32),
                pltpu.VMEM((8, width), f32),
                pltpu.VMEM((8, width), f32),
                pltpu.VMEM((blocks, 8, width), f32),
                dma((2,)),
                dma((blocks - 1,)), dma((blocks - 1,)),
                dma((groups - 2,)), dma((1,)),
                dma((blocks,)), dma((blocks,)),
                dma((1,)), dma((1,)),
                dma((2 * blocks - 2,)), dma((2 * blocks - 2,)),
                dma((1,)), dma((1,)),
                dma((2,)), dma((groups,)),
                dma((groups - 1,)), dma((1,)),
                dma((blocks - 1,)), dma((blocks - 1,)),
            ],
            compiler_params=pltpu.CompilerParams(
                collective_id=0, has_side_effects=True, vmem_limit_bytes=60 * 1024 * 1024
            ),
        )(spreads, embeddings.reshape(1, 2, half, width))
        return mmd, gradient

    return jax.shard_map(
        shards,
        mesh=mesh,
        in_specs=(P("var", "blk", None), P()),
        out_specs=(P("var"), P("var", "blk", None)),
        check_vma=False,
    )
```

time: 24.1 us -> 22.4 us (0.929)
  Pallas kernels: 19.4 us -> 18.3 us
  local copies, waits for them, and re-layouts: 2.12 us -> 1.47 us
    pallas_call x1, Pallas kernels: 19.4 us -> 18.3 us  [shards(): pl.pallas_call(functools.partial(kernel, groups, blocks, bands), out_shap...]
    unnamed x5 -> x1, local copies, waits for them, and re-layouts: 2.12 us -> 1.47 us
where the time goes in v2:
time: 22.4 us; the launch traced here: 22.2 us
  Pallas kernels  18.3 us (82%)
  between operations  2.38 us (11%)
  local copies, waits for them, and re-layouts  1.47 us (7%)
    pallas_call x1, Pallas kernels, shards(): pl.pallas_call(functools.partial(kernel, groups, blocks, bands), out_shap...  18.3 us
    unnamed x1, local copies, waits for them, and re-layouts  1.47 us

profile of v2, /device:TPU:0, one launch (start us, length us, event | category | flops | bytes accessed | tf_op | source)
XLA Modules:
  0.0 22.2 jit_solution(4457333485166962877)
XLA Ops:
  0.6 18.3 %shard_map.41 = (f32[1]{0:T(128)}, f32[1,128,128]{2,1,0:T(8,128)}) custom-call(f32[5]{0:T(128)} %spread_hbm.1, f32[1,2,64,128]{3,2,1,0:T(8,128)} %bitcast.1), custom_call_target="tpu_custom_call" | custom-call | tf_op jit(solution)/shard_map/pallas_call | solution.py:333
  19.6 1.5 %copy.7 = f32[1,128,128]{2,1,0:T(8,128)} copy(f32[1,128,128]{2,1,0:T(8,128)} %get-tuple-element.5) | data formatting | bytes 131072

commit v3 on v2

--- a/solution.py
+++ b/solution.py
@@ -9,7 +9,8 @@
 
 HIGHEST = lax.Precision.HIGHEST
 LOG2E = 1.4426950408889634
-EARLY = 2
+LEFT = (0, 0, 1, 0, 1, 2)
+RIGHT = (0, 1, 0, 2, 1, 0)
 
 
 def partner(index, step, count):
@@ -33,6 +34,19 @@
     )
 
 
+def pieces(rows):
+    high = rows.astype(jnp.bfloat16)
+    rest = rows - high.astype(jnp.float32)
+    mid = rest.astype(jnp.bfloat16)
+    return high, mid, (rest - mid.astype(jnp.float32)).astype(jnp.bfloat16)
+
+
+def matmul(left, right, right_dim):
+    return lax.dot_general(
+        left, right, (((1,), (right_dim,)), ((), ())), preferred_element_type=jnp.float32
+    )
+
+
 def fold(tile):
     return jnp.sum(tile.reshape(tile.shape[0] // 8, 8, tile.shape[1]), axis=0)
 
@@ -48,7 +62,7 @@
 def kernel(
     groups, blocks, bands,
     spread_hbm, emb_hbm, mmd_ref, grad_ref,
-    spread_ref, own_ref, y_buf, x_buf, t_buf, t_out, t_mate, s_buf, s_out, m_buf,
+    spread_ref, own_ref, y_buf, x_buf, t_buf, t_out, t_mate, s_buf, s_out, m_buf, y_pack, y_sq,
     load, y_send, y_recv, x_send, x_recv, n_send, n_recv, w_send, w_recv, g_send, g_recv,
     p_send, p_recv, t_send, t_recv, s_send, s_recv, m_send, m_recv,
 ):
@@ -164,7 +178,9 @@
     own_col = col_square(own)
 
     def tile(left, left_row, right, right_col, sums):
-        distance = left_row + right_col - 2.0 * dot_t(left, right)
+        return bands_of(left_row + right_col - 2.0 * dot_t(left, right), sums)
+
+    def bands_of(distance, sums):
         total = None
         weights = None
         for gain, rate in zip(gains, rates):
@@ -178,28 +194,42 @@
     def y_block(step):
         return own if step == 0 else whole(y_buf[step - 1])
 
-    def y_col(step):
-        return own_col if step == 0 else col_square(y_block(step))
+    def pack_group():
+        for step in range(blocks):
+            rows = y_block(step)
+            terms = pieces(rows)
+            span = pl.ds(step * count, count)
+            for place, index in enumerate(RIGHT):
+                y_pack[span, pl.ds(place * width, width)] = terms[index]
+            y_sq[:, span] = dot_t(jnp.ones((8, width), jnp.float32), rows * rows)
+
+    def against_packed(left):
+        terms = pieces(left)
+        left_row = row_square(left)
+        inner = matmul(jnp.concatenate([terms[index] for index in LEFT], axis=1), y_pack[...], 1)
+        total, weights = None, []
+        for step in range(blocks):
+            span = slice(step * count, (step + 1) * count)
+            part, w = bands_of(left_row + y_sq[0:1, span] - 2.0 * inner[:, span], True)
+            total = part if total is None else total + part
+            weights.append(w)
+        row = functools.reduce(jnp.add, weights)
+        high, mid, low = pieces(jnp.concatenate(weights, axis=1))
+        mix = matmul(high, y_pack[:, RIGHT.index(2) * width:(RIGHT.index(2) + 1) * width], 0)
+        mix = mix + matmul(low, y_pack[:, 0:width], 0)
+        both = matmul(jnp.concatenate([high, mid], axis=0), y_pack[:, 0:2 * width], 0)
+        size = left.shape[0]
+        mix = mix + both[size:, width:] + both[size:, :width] + both[:size, width:] + both[:size, :width]
+        return total, row, mix
 
     def add(state, term):
         return term if state is None else tuple(a + b for a, b in zip(state, term))
 
-    def against_group(left, left_row, steps, state=None, wait=False):
-        for step in steps:
-            if wait and step:
-                y_copy(step).wait_recv()
-            rows = y_block(step)
-            part, w = tile(left, left_row, rows, y_col(step), True)
-            state = add(state, (part, w, dot_n(w, rows)))
-        return state
-
     def difference(weights, rows, mix):
         return jnp.sum(weights, axis=1, keepdims=True) * rows - mix
 
-    self_state = against_group(own, own_row, range(EARLY), None, True)
-
     def rest_of_self():
-        total, weights, mix = against_group(own, own_row, range(EARLY, blocks), self_state)
+        total, weights, mix = against_packed(own)
         return total, -4.0 * difference(weights, own, mix)
 
     def finish_mmd(part):
@@ -214,8 +244,9 @@
 
     @pl.when(nominal)
     def _():
-        for step in range(EARLY, blocks):
+        for step in range(1, blocks):
             y_copy(step).wait_recv()
+        pack_group()
         total, self_grad = rest_of_self()
         s_out[...] = total
         for var in range(1, groups):
@@ -237,6 +268,10 @@
 
     @pl.when(jnp.logical_not(nominal))
     def _():
+        for step in range(1, blocks):
+            y_copy(step).wait_recv()
+        pack_group()
+
         @pl.when(outer)
         def _():
             x_copy(group, core).wait_recv()
@@ -249,12 +284,9 @@
         def _():
             n_copy(0).wait_recv()
 
-        for step in range(EARLY, blocks):
-            y_copy(step).wait_recv()
-
         def cross(part):
             anchor = x_buf[0, part]
-            total, weights, mix = against_group(anchor, row_square(anchor), range(blocks))
+            total, weights, mix = against_packed(anchor)
             return total, -2.0 * difference(weights, anchor, mix)
 
         first_total, t_out[core] = cross(core)
@@ -346,6 +378,8 @@
                 pltpu.VMEM((8, width), f32),
                 pltpu.VMEM((8, width), f32),
                 pltpu.VMEM((blocks, 8, width), f32),
+                pltpu.VMEM((blocks * count, len(RIGHT) * width), jnp.bfloat16),
+                pltpu.VMEM((8, blocks * count), f32),
                 dma((2,)),
                 dma((blocks - 1,)), dma((blocks - 1,)),
                 dma((groups - 2,)), dma((1,)),
@@ -358,9 +392,12 @@
                 dma((blocks - 1,)), dma((blocks - 1,)),
             ],
             compiler_params=pltpu.CompilerParams(
-                collective_id=0, has_side_effects=True, vmem_limit_bytes=60 * 1024 * 1024
+                collective_id=0, has_side_effects=True, vmem_limit_bytes=32 * 1024 * 1024
             ),
-        )(spreads, embeddings.reshape(1, 2, half, width))
+        )(
+            pltpu.with_memory_space_constraint(spreads, pltpu.HBM),
+            pltpu.with_memory_space_constraint(embeddings.reshape(1, 2, half, width), pltpu.HBM),
+        )
         return mmd, gradient
 
     return jax.shard_map(

time: 22.4 us -> 20.2 us (0.902)
  Pallas kernels: 18.3 us -> 17.1 us
  local copies, waits for them, and re-layouts: 1.47 us -> 0.63 us
    pallas_call x1, Pallas kernels: 18.3 us -> 17.1 us  [shards(): pl.pallas_call(functools.partial(kernel, groups, blocks, bands), out_shap...]
    unnamed x1, local copies, waits for them, and re-layouts: 1.47 us -> 0.63 us
where the time goes in v3:
time: 20.2 us; the launch traced here: 20.1 us
  Pallas kernels  17.1 us (85%)
  between operations  2.32 us (11%)
  local copies, waits for them, and re-layouts  0.63 us (3%)
    pallas_call x1, Pallas kernels, shards(): pl.pallas_call(functools.partial(kernel, groups, blocks, bands), out_shap...  17.1 us
    unnamed x1, local copies, waits for them, and re-layouts  0.63 us

profile of v3, /device:TPU:0, one launch (start us, length us, event | category | flops | bytes accessed | tf_op | source)
XLA Modules:
  0.0 20.1 jit_solution(14280266953468978681)
XLA Ops:
  0.6 17.1 %shard_map.41 = (f32[1]{0:T(128)}, f32[1,128,128]{2,1,0:T(8,128)S(1)}) custom-call(f32[5]{0:T(128)} %spread_hbm.1, f32[1,2,64,128]{3,2,1,0:T(8,128)} %bitcast.1), custom_call_target="tpu_custom_call" | custom-call | tf_op jit(solution)/shard_map/pallas_call | solution.py:365
  18.3 0.6 %copy.7 = f32[1,128,128]{2,1,0:T(8,128)} copy(f32[1,128,128]{2,1,0:T(8,128)S(1)} %get-tuple-element.5) | data formatting | bytes 131072
